TPU v7x, 512 devices: a whole 4x8x8 slice. The times are simulated.
512 devices in a mesh: head: 8 (over y), seq: 64 (over z, x, core).
Axes of the slice: x: 4, y: 8, z: 8, core: 2. Of those that a mesh axis runs over, the one named last changes fastest.
Arguments:
- q_in: bfloat16 [16384, 3072], P('seq', 'head'), may hold values from -32 to 32
- k_in: bfloat16 [16384, 3072], P('seq', 'head'), may hold values from -32 to 32
- v_in: bfloat16 [16384, 3072], P('seq', 'head'), may hold values from -6 to 6
- q_rank: int32 [2, 24, 16384], P(None, 'head', 'seq'), may hold values from 0 to 16383, as said below
- k_rank: int32 [2, 24, 16384], P(None, 'head', 'seq'), may hold values from 0 to 16383, as said below
- w_out: bfloat16 [3072, 3072], P(None, 'head'), may hold values from -0.109375 to 0.109375
Outputs:
- mixed: bfloat16 [16384, 3072], P('seq', 'head')
Inputs may be any that keep to these rules, and one draw needn't show every extreme that they name: Each row q_rank[r, h, :] is a permutation of the 16384 positions; for every round, head and pair of seq shards s and d, at most 8 tokens of shard s have positions from d * 256 to (d + 1) * 256 - 1, and for every round, head and seq shard s, some shard d receives exactly 8 tokens of s. `k_rank`: as for q_rank, independently drawn.
All inputs are finite; a program needn't handle non-finite values.
Results may differ from a plain program's by a relative error of at most 0.0064.
Values may be sent and summed in bfloat16 or wider, within the bound.
A program may use at most 64 MiB of HBM per device.

v0:
```python
import functools

import jax
import jax.numpy as jnp
from jax import lax
from jax.experimental import pallas as pl
from jax.experimental.pallas import tpu as pltpu
from jax.sharding import PartitionSpec as P

MESH = pl.DeviceIdType.MESH
HD = 128
EMPTY = 64.0
F32 = jnp.float32
BF16 = jnp.bfloat16


def dot(a, b, dims=((1,), (0,)), precision=None):
    return lax.dot_general(a, b, (dims, ((), ())), preferred_element_type=F32, precision=precision)


def kernel(
    sizes, q_ref, k_ref, v_ref, qrank_ref, krank_ref, w_hbm, out_ref,
    w_ref, send_x, recv_x, send_o, recv_o, send_l, recv_l, gath, pq_ref, tq_ref, oq_ref,
    w_sem, sx_sem, rx_sem, so_sem, ro_sem, sl_sem, rl_sem, sg_sem, rg_sem,
):
    nseq, nhead, per, rounds, length = sizes
    cap = 2 * length // nseq
    slots = nseq * cap
    me = lax.axis_index("seq")
    my_head = lax.axis_index("head")
    barrier = pltpu.get_barrier_semaphore()

    def peer_of(step):
        outer = 8 if nseq % 8 == 0 else 1
        inner = nseq // outer
        hop, rest = step % outer, step // outer
        return ((me // inner + hop) % outer) * inner + (me % inner + rest) % inner

    @pl.loop(1, nseq)
    def _(step):
        pl.semaphore_signal(barrier, inc=1, device_id={"seq": peer_of(step)}, device_id_type=MESH)

    @pl.loop(1, nhead)
    def _(step):
        pl.semaphore_signal(barrier, inc=1, device_id={"head": (my_head + step) % nhead}, device_id_type=MESH)

    w_copy = pltpu.make_async_copy(w_hbm, w_ref, w_sem)
    w_copy.start()

    shard_ids = lax.broadcasted_iota(jnp.int32, (nseq, length), 0)
    slot_ids = lax.broadcasted_iota(jnp.int32, (slots, length), 0)
    earlier = (
        lax.broadcasted_iota(jnp.int32, (length, length), 0) < lax.broadcasted_iota(jnp.int32, (length, length), 1)
    ).astype(F32).astype(BF16)

    def route(rank_row):
        target = rank_row // length
        owner = (target == shard_ids).astype(F32)
        before = dot(owner.astype(BF16), earlier)
        ordinal = jnp.sum(owner * before, axis=0, keepdims=True)
        slot = target * cap + ordinal.astype(jnp.int32)
        place = (slot_ids == slot).astype(F32).astype(BF16)
        return owner, ordinal, place, jnp.sum(owner, axis=1, keepdims=True)

    def by_peer(rows):
        return rows.reshape(nseq, cap, HD)

    def pack(h):
        cols = slice(h * HD, (h + 1) * HD)
        q_rows, k_rows, v_rows = [], [], []
        for r in range(rounds):
            owner, ordinal, place, _ = route(qrank_ref[r, h : h + 1, :])
            pq_ref[r, h] = place
            tq_ref[r, h] = owner
            oq_ref[r, h] = ordinal
            q_rows.append(by_peer(dot(place, q_ref[:, cols])))
            _, _, place, count = route(krank_ref[r, h : h + 1, :])
            both = dot(place, jnp.concatenate([k_ref[:, cols], v_ref[:, cols]], axis=1))
            seat = lax.broadcasted_iota(jnp.int32, (nseq, cap, HD), 1).astype(F32)
            filled = seat < jnp.broadcast_to(count, (nseq, HD))[:, None, :]
            k_rows.append(jnp.where(filled, by_peer(both[:, :HD]), EMPTY))
            v_rows.append(by_peer(both[:, HD:]))
        for i, rows in enumerate((q_rows, k_rows, v_rows)):
            send_x[h, :, i] = jnp.concatenate(rows, axis=1).astype(BF16)

    def push(send, recv, send_sem, recv_sem, h):
        recv[h, me] = send[h, me]

        @pl.loop(1, nseq)
        def _(step):
            peer = peer_of(step)
            pltpu.make_async_remote_copy(
                src_ref=send.at[h, peer],
                dst_ref=recv.at[h, me],
                send_sem=send_sem.at[h],
                recv_sem=recv_sem.at[h],
                device_id={"seq": peer},
                device_id_type=MESH,
            ).start()

    def await_all(buf, sem, h):
        part = buf.at[h, pl.ds(0, nseq - 1)]
        pltpu.make_async_copy(part, part, sem.at[h]).wait()

    def attend(h):
        lane = lax.broadcasted_iota(jnp.int32, (slots, HD), 1)
        row = lax.broadcasted_iota(jnp.int32, (slots, HD), 0)
        column_shard = lax.broadcasted_iota(jnp.int32, (nseq, slots), 1) // cap
        same_shard = column_shard == lax.broadcasted_iota(jnp.int32, (nseq, slots), 0)
        block = slots // 2
        out_rows = []
        logs = jnp.zeros((nseq, HD), F32)
        for r in range(rounds):

            def half(i):
                tile = recv_x[h, :, i].astype(F32)
                return tile[:, r * cap : (r + 1) * cap].reshape(slots, HD)

            q_all = half(0).astype(BF16)
            k_all = half(1)
            empty = k_all > 0.5 * EMPTY
            k_all = k_all.astype(BF16)
            v_all = half(2).astype(BF16)
            empty = jnp.concatenate([empty.astype(F32)] * (block // HD), axis=1) > 0.5 if block > HD else empty[:, :block]
            parts, log_parts = [], []
            for c in range(2):
                scores = dot(k_all, q_all[c * block : (c + 1) * block], ((1,), (1,))) * HD ** (-0.5)
                scores = jnp.where(empty, -1e30, scores)
                peak = jnp.max(scores, axis=0, keepdims=True)
                weights = jnp.exp(scores - peak)
                total = jnp.sum(weights, axis=0, keepdims=True)
                weights = (weights * (1.0 / total)).astype(BF16)
                parts.append(dot(v_all, weights, ((0,), (0,))).T)
                log_parts.append(peak + jnp.log(total))
            out_rows.append(by_peer(jnp.concatenate(parts, axis=0)))
            log_row = jnp.concatenate(log_parts, axis=1)
            spread = jnp.where(same_shard, log_row, 0.0)
            seat = (lane == row % cap + r * cap).astype(F32)
            logs = logs + dot(spread, seat, precision=lax.Precision.HIGHEST)
        send_o[h] = jnp.concatenate(out_rows, axis=1).astype(BF16)
        for d in range(nseq):
            send_l[h, d] = logs[d : d + 1]

    def mix(h):
        logs_in = jnp.concatenate([recv_l[h, d] for d in range(nseq)], axis=0)
        seat = lax.broadcasted_iota(jnp.int32, (cap, length), 0).astype(F32)
        logs, rows = [], []
        tile = recv_o[h].astype(F32)
        for r in range(rounds):
            of_owner = dot(logs_in, tq_ref[r, h], ((0,), (0,)), precision=lax.Precision.HIGHEST)
            mine = jnp.where(seat == oq_ref[r, h], of_owner[r * cap : (r + 1) * cap], 0.0)
            logs.append(jnp.sum(mine, axis=0, keepdims=True))
            part = tile[:, r * cap : (r + 1) * cap].reshape(slots, HD).astype(BF16)
            rows.append(dot(part, pq_ref[r, h], ((0,), (0,))))
        peak = functools.reduce(jnp.maximum, logs)
        shares = [jnp.exp(log - peak) for log in logs]
        total = functools.reduce(jnp.add, shares)
        mixed = functools.reduce(jnp.add, [share / total * row for share, row in zip(shares, rows)])
        gath[h, my_head] = mixed.T.astype(BF16)

    def push_heads(h):
        @pl.loop(1, nhead)
        def _(step):
            pltpu.make_async_remote_copy(
                src_ref=gath.at[h, my_head],
                dst_ref=gath.at[h, my_head],
                send_sem=sg_sem.at[h],
                recv_sem=rg_sem.at[h],
                device_id={"head": (my_head + step) % nhead},
                device_id_type=MESH,
            ).start()

    def await_heads(sem, h):
        part = gath.at[h, pl.ds(0, nhead - 1)]
        pltpu.make_async_copy(part, part, sem.at[h]).wait()

    for h in range(per):
        pack(h)
        if h == 0:
            pl.semaphore_wait(barrier, nseq + nhead - 2)
        push(send_x, recv_x, sx_sem, rx_sem, h)
    for h in range(per):
        await_all(recv_x, rx_sem, h)
        attend(h)
        push(send_o, recv_o, so_sem, ro_sem, h)
        push(send_l, recv_l, sl_sem, rl_sem, h)
    for h in range(per):
        await_all(recv_o, ro_sem, h)
        await_all(recv_l, rl_sem, h)
        mix(h)
        push_heads(h)
    w_copy.wait()
    total = None
    for h in range(per):
        await_heads(rg_sem, h)
        left = jnp.concatenate([gath[h, y] for y in range(nhead)], axis=1)
        right = jnp.concatenate([w_ref[(y * per + h) * HD : (y * per + h + 1) * HD] for y in range(nhead)], axis=0)
        part = dot(left, right)
        total = part if total is None else total + part
    out_ref[...] = total.astype(BF16)
    for h in range(per):
        await_all(send_x, sx_sem, h)
        await_all(send_o, so_sem, h)
        await_all(send_l, sl_sem, h)
        await_heads(sg_sem, h)


def solution(mesh):
    nseq, nhead = mesh.shape["seq"], mesh.shape["head"]

    def body(q_in, k_in, v_in, q_rank, k_rank, w_out):
        length, width = q_in.shape
        rounds, per, _ = q_rank.shape
        cap = 2 * length // nseq
        slots = nseq * cap
        vmem = pl.BlockSpec(memory_space=pltpu.VMEM)
        scratch = [
            pltpu.VMEM(w_out.shape, BF16),
            pltpu.VMEM((per, nseq, 3, rounds * cap, HD), BF16),
            pltpu.VMEM((per, nseq, 3, rounds * cap, HD), BF16),
            pltpu.VMEM((per, nseq, rounds * cap, HD), BF16),
            pltpu.VMEM((per, nseq, rounds * cap, HD), BF16),
            pltpu.VMEM((per, nseq, 1, HD), F32),
            pltpu.VMEM((per, nseq, 1, HD), F32),
            pltpu.VMEM((per, nhead, length, HD), BF16),
            pltpu.VMEM((rounds, per, slots, length), BF16),
            pltpu.VMEM((rounds, per, nseq, length), F32),
            pltpu.VMEM((rounds, per, 1, length), F32),
            pltpu.SemaphoreType.DMA,
        ] + [pltpu.SemaphoreType.DMA((per,))] * 8
        return pl.pallas_call(
            functools.partial(kernel, (nseq, nhead, per, rounds, length)),
            out_shape=jax.ShapeDtypeStruct((length, w_out.shape[1]), BF16),
            in_specs=[vmem] * 5 + [pl.BlockSpec(memory_space=pl.ANY)],
            out_specs=vmem,
            scratch_shapes=scratch,
            compiler_params=pltpu.CompilerParams(
                collective_id=0, has_side_effects=True, vmem_limit_bytes=48 * 1024 * 1024
            ),
        )(q_in, k_in, v_in, q_rank, k_rank, w_out)

    return jax.shard_map(
        body,
        mesh=mesh,
        in_specs=(
            P("seq", "head"),
            P("seq", "head"),
            P("seq", "head"),
            P(None, "head", "seq"),
            P(None, "head", "seq"),
            P(None, "head"),
        ),
        out_specs=P("seq", "head"),
        check_vma=False,
    )
```

profile of v0, /device:TPU:1, one launch (start us, length us, event | category | flops | bytes accessed | tf_op | source)
XLA Modules:
  0.0 122.5 jit_solution(1244016926043261216)
XLA Ops:
  0.0 0.7 copy.7.qrank_ref
  0.7 0.7 copy.8.krank_ref
  1.4 0.0 copy-start
  1.4 1.7 %copy-done = bf16[3072,384]{1,0:T(8,128)(2,1)S(1)} copy-done((bf16[3072,384]{1,0:T(8,128)(2,1)S(1)}, bf16[3072,384]{1,0:T(8,128)(2,1)}, u32[]{:S(2)}) %copy-start) | copy-done | bytes 2359320
  3.1 0.0 copy-start.1
  3.1 0.9 copy-done.1
  4.0 0.0 copy-start.2
  4.0 0.9 copy-done.2
  4.9 0.0 copy-start.3
  4.9 0.9 copy-done.3
  5.8 116.0 %shard_map.64 = bf16[256,384]{1,0:T(8,128)(2,1)S(1)} custom-call(bf16[256,384]{1,0:T(8,128)(2,1)S(1)} %copy-done.1, bf16[256,384]{1,0:T(8,128)(2,1)S(1)} %copy-done.2, bf16[256,384]{1,0:T(8,128)(2,1)S(1)} %copy-done.3, s32[2,3,256]{2,1,0:T(4,128)S(1)} %copy.7.qrank_ref, s32[2,3,256]{2,1,0:T(4,128)S(1)} %copy.8.krank_ref, bf16[3072,384]{1,0:T(8,128)(2,1)S(1)} %copy-done), custom_call_target="tpu_custom_call" | custom-call | tf_op jit(solution)/shard_map/pallas_call | solution.py:231
  121.9 0.7 copy.10
Async XLA Ops:
  1.4 1.7 %copy-start = (bf16[3072,384]{1,0:T(8,128)(2,1)S(1)}, bf16[3072,384]{1,0:T(8,128)(2,1)}, u32[]{:S(2)}) copy-start(bf16[3072,384]{1,0:T(8,128)(2,1)} %w_hbm.1) | copy-start | bytes 7077892
  3.1 0.9 copy-start.1
  4.0 0.9 copy-start.2
  4.9 0.9 copy-start.3
where the time goes:
time: 123 us
  Pallas kernels  116 us (94%)
  local copies, waits for them, and re-layouts  6.51 us (5%)
    pallas_call x1, Pallas kernels, body(): pl.pallas_call(functools.partial(kernel, (nseq, nhead, per, rounds, lengt...  116 us
    unnamed x11, local copies, waits for them, and re-layouts  6.51 us

commit v1 on v0

--- a/solution.py
+++ b/solution.py
@@ -9,6 +9,7 @@
 
 MESH = pl.DeviceIdType.MESH
 HD = 128
+PLANES = 8
 EMPTY = 64.0
 F32 = jnp.float32
 BF16 = jnp.bfloat16
@@ -19,22 +20,25 @@
 
 
 def kernel(
-    sizes, q_ref, k_ref, v_ref, qrank_ref, krank_ref, w_hbm, out_ref,
-    w_ref, send_x, recv_x, send_o, recv_o, send_l, recv_l, gath, pq_ref, tq_ref, oq_ref,
-    w_sem, sx_sem, rx_sem, so_sem, ro_sem, sl_sem, rl_sem, sg_sem, rg_sem,
+    sizes, q_hbm, k_hbm, v_hbm, qrank_ref, krank_ref, w_hbm, out_ref,
+    w_ref, shard, seats, packed, recv_x, send_o, recv_o, send_l, recv_l, gath, tq_ref, oq_ref,
+    w_sem, seat_send, seat_recv, ring_send, ring_recv,
+    sx_sem, rx_sem, so_sem, ro_sem, sl_sem, rl_sem, sg_sem, rg_sem,
 ):
     nseq, nhead, per, rounds, length = sizes
     cap = 2 * length // nseq
     slots = nseq * cap
+    inner = nseq // PLANES
     me = lax.axis_index("seq")
     my_head = lax.axis_index("head")
+    my_plane, my_place = me // inner, me % inner
     barrier = pltpu.get_barrier_semaphore()
 
+    def plane_at(hop):
+        return (my_plane + hop + PLANES) % PLANES
+
     def peer_of(step):
-        outer = 8 if nseq % 8 == 0 else 1
-        inner = nseq // outer
-        hop, rest = step % outer, step // outer
-        return ((me // inner + hop) % outer) * inner + (me % inner + rest) % inner
+        return plane_at(step % PLANES) * inner + (my_place + step // PLANES) % inner
 
     @pl.loop(1, nseq)
     def _(step):
@@ -44,44 +48,130 @@
     def _(step):
         pl.semaphore_signal(barrier, inc=1, device_id={"head": (my_head + step) % nhead}, device_id_type=MESH)
 
+    for h in range(per):
+        for i, source in enumerate((q_hbm, k_hbm, v_hbm)):
+            pltpu.make_async_copy(source.at[:, pl.ds(h * HD, HD)], shard.at[h, 0, i], ring_recv.at[h, 0]).start()
     w_copy = pltpu.make_async_copy(w_hbm, w_ref, w_sem)
     w_copy.start()
 
-    shard_ids = lax.broadcasted_iota(jnp.int32, (nseq, length), 0)
-    slot_ids = lax.broadcasted_iota(jnp.int32, (slots, length), 0)
-    earlier = (
-        lax.broadcasted_iota(jnp.int32, (length, length), 0) < lax.broadcasted_iota(jnp.int32, (length, length), 1)
-    ).astype(F32).astype(BF16)
-
-    def route(rank_row):
-        target = rank_row // length
-        owner = (target == shard_ids).astype(F32)
-        before = dot(owner.astype(BF16), earlier)
-        ordinal = jnp.sum(owner * before, axis=0, keepdims=True)
-        slot = target * cap + ordinal.astype(jnp.int32)
-        place = (slot_ids == slot).astype(F32).astype(BF16)
-        return owner, ordinal, place, jnp.sum(owner, axis=1, keepdims=True)
+    def find_seats():
+        shard_ids = lax.broadcasted_iota(jnp.int32, (nseq, length), 0)
+        earlier = (
+            lax.broadcasted_iota(jnp.int32, (length, length), 0)
+            < lax.broadcasted_iota(jnp.int32, (length, length), 1)
+        ).astype(F32).astype(BF16)
+        seats[0] = jnp.zeros(seats.shape[1:], F32)
+        for side, rank_ref in enumerate((qrank_ref, krank_ref)):
+            for r in range(rounds):
+                for h in range(per):
+                    target = rank_ref[r, h : h + 1, :] // length
+                    owner = (target == shard_ids).astype(F32)
+                    before = dot(owner.astype(BF16), earlier)
+                    ordinal = jnp.sum(owner * before, axis=0, keepdims=True)
+                    row = (side * rounds + r) * per + h
+                    seats[0, row : row + 1] = (target * cap).astype(F32) + ordinal
+                    if side == 0:
+                        tq_ref[r, h] = owner
+                        oq_ref[r, h] = ordinal
+
+    def seat_row(j, side, r, h):
+        row = (side * rounds + r) * per + h
+        return seats[j, row : row + 1].astype(jnp.int32)
+
+    def ring(buf, h, send_sem, recv_sem, source, target, hop):
+        at = (lambda j: buf.at[j]) if h is None else (lambda j: buf.at[h, j])
+        pltpu.make_async_remote_copy(
+            src_ref=at(source),
+            dst_ref=at(target),
+            send_sem=send_sem,
+            recv_sem=recv_sem.at[target] if h is None else recv_sem.at[h, target],
+            device_id={"seq": plane_at(hop) * inner + my_place},
+            device_id_type=MESH,
+        ).start()
+
+    def ring_shards(h, stage):
+        for (source, target), hop in zip(((0, 1), (0, 2)) if stage == 0 else ((1, 3), (2, 4)), (1, -1)):
+            ring(shard, h, ring_send.at[h], ring_recv, source, target, hop)
+
+    def ring_seats(stage):
+        for (source, target), hop in zip(((0, 1), (0, 2)) if stage == 0 else ((1, 3), (2, 4)), (1, -1)):
+            ring(seats, None, seat_send, seat_recv, source, target, hop)
+
+    def await_shard(h, j):
+        pltpu.make_async_copy(shard.at[h, j], shard.at[h, j], ring_recv.at[h, j]).wait()
+
+    def await_seats(j):
+        pltpu.make_async_copy(seats.at[j], seats.at[j], seat_recv.at[j]).wait()
+
+    def pack(h, j, targets):
+        n = len(targets) * inner
+        ids = [lax.broadcasted_iota(jnp.int32, (inner * cap, length), 0) + plane * (inner * cap) for plane, _ in targets]
+        ids = jnp.concatenate(ids, axis=0)
+        q_all = shard[h, j, 0]
+        kv_all = jnp.concatenate([shard[h, j, 1], shard[h, j, 2]], axis=1)
+        q_rows, k_rows, v_rows = [], [], []
+        for r in range(rounds):
+            place = (ids == seat_row(j, 0, r, h)).astype(F32).astype(BF16)
+            q_rows.append(dot(place, q_all).reshape(n, cap, HD))
+            place = (ids == seat_row(j, 1, r, h)).astype(F32)
+            filled = jnp.sum(place, axis=1, keepdims=True) > 0.5
+            both = dot(place.astype(BF16), kv_all)
+            k_rows.append(jnp.where(filled, both[:, :HD], EMPTY).reshape(n, cap, HD))
+            v_rows.append(both[:, HD:].reshape(n, cap, HD))
+        for i, rows in enumerate((q_rows, k_rows, v_rows)):
+            rows = jnp.concatenate(rows, axis=1).astype(BF16)
+            for t, (_, index) in enumerate(targets):
+                packed[h, index, :, i] = rows[t * inner : (t + 1) * inner]
+
+    def deliver(h, index, place, plane, source):
+        pltpu.make_async_remote_copy(
+            src_ref=packed.at[h, index, place],
+            dst_ref=recv_x.at[h, source],
+            send_sem=sx_sem.at[h],
+            recv_sem=rx_sem.at[h],
+            device_id={"seq": plane * inner + place},
+            device_id_type=MESH,
+        ).start()
+
+    def near(h, js):
+        for j in js:
+            source = plane_at((0, -1, 1, -2, 2)[j]) * inner + my_place
+            pack(h, j, [(my_plane, j)])
+            recv_x[h, source] = packed[h, j, my_place]
+
+            @pl.loop(1, inner)
+            def _(step):
+                deliver(h, j, (my_place + step) % inner, my_plane, source)
+
+    def relay(h):
+        for j, way in ((3, 1), (4, -1)):
+            source = plane_at(-2 * way) * inner + my_place
+            one, two = 2 * j - 1, 2 * j
+            pack(h, j, [(my_plane, j), (plane_at(way), one), (plane_at(2 * way), two)])
+
+            @pl.loop(0, inner)
+            def _(step):
+                deliver(h, one, (my_place + step) % inner, plane_at(way), source)
+
+            odd = j - 3
+            half = (inner + 1 - odd) // 2
+
+            @pl.loop(0, half)
+            def _(step):
+                deliver(h, two, 2 * ((my_place // 2 + step) % half) + odd, plane_at(2 * way), source)
+
+            recv_x[h, source] = packed[h, j, my_place]
+
+            @pl.loop(1, inner)
+            def _(step):
+                deliver(h, j, (my_place + step) % inner, my_plane, source)
+
+    def await_rows(buf, sem, h):
+        part = recv_x.at[h, pl.ds(0, nseq - 5)]
+        pltpu.make_async_copy(part, part, sem.at[h]).wait()
 
     def by_peer(rows):
         return rows.reshape(nseq, cap, HD)
-
-    def pack(h):
-        cols = slice(h * HD, (h + 1) * HD)
-        q_rows, k_rows, v_rows = [], [], []
-        for r in range(rounds):
-            owner, ordinal, place, _ = route(qrank_ref[r, h : h + 1, :])
-            pq_ref[r, h] = place
-            tq_ref[r, h] = owner
-            oq_ref[r, h] = ordinal
-            q_rows.append(by_peer(dot(place, q_ref[:, cols])))
-            _, _, place, count = route(krank_ref[r, h : h + 1, :])
-            both = dot(place, jnp.concatenate([k_ref[:, cols], v_ref[:, cols]], axis=1))
-            seat = lax.broadcasted_iota(jnp.int32, (nseq, cap, HD), 1).astype(F32)
-            filled = seat < jnp.broadcast_to(count, (nseq, HD))[:, None, :]
-            k_rows.append(jnp.where(filled, by_peer(both[:, :HD]), EMPTY))
-            v_rows.append(by_peer(both[:, HD:]))
-        for i, rows in enumerate((q_rows, k_rows, v_rows)):
-            send_x[h, :, i] = jnp.concatenate(rows, axis=1).astype(BF16)
 
     def push(send, recv, send_sem, recv_sem, h):
         recv[h, me] = send[h, me]
@@ -146,12 +236,14 @@
         seat = lax.broadcasted_iota(jnp.int32, (cap, length), 0).astype(F32)
         logs, rows = [], []
         tile = recv_o[h].astype(F32)
+        slot_ids = lax.broadcasted_iota(jnp.int32, (slots, length), 0)
         for r in range(rounds):
             of_owner = dot(logs_in, tq_ref[r, h], ((0,), (0,)), precision=lax.Precision.HIGHEST)
             mine = jnp.where(seat == oq_ref[r, h], of_owner[r * cap : (r + 1) * cap], 0.0)
             logs.append(jnp.sum(mine, axis=0, keepdims=True))
             part = tile[:, r * cap : (r + 1) * cap].reshape(slots, HD).astype(BF16)
-            rows.append(dot(part, pq_ref[r, h], ((0,), (0,))))
+            place = (slot_ids == seat_row(0, 0, r, h)).astype(F32).astype(BF16)
+            rows.append(dot(part, place, ((0,), (0,))))
         peak = functools.reduce(jnp.maximum, logs)
         shares = [jnp.exp(log - peak) for log in logs]
         total = functools.reduce(jnp.add, shares)
@@ -159,6 +251,8 @@
         gath[h, my_head] = mixed.T.astype(BF16)
 
     def push_heads(h):
+        if nhead == 1:
+            return
         @pl.loop(1, nhead)
         def _(step):
             pltpu.make_async_remote_copy(
@@ -171,35 +265,82 @@
             ).start()
 
     def await_heads(sem, h):
+        if nhead == 1:
+            return
         part = gath.at[h, pl.ds(0, nhead - 1)]
         pltpu.make_async_copy(part, part, sem.at[h]).wait()
 
-    for h in range(per):
-        pack(h)
-        if h == 0:
-            pl.semaphore_wait(barrier, nseq + nhead - 2)
-        push(send_x, recv_x, sx_sem, rx_sem, h)
-    for h in range(per):
-        await_all(recv_x, rx_sem, h)
+    def project(h):
+        left = jnp.concatenate([gath[h, y] for y in range(nhead)], axis=1)
+        right = jnp.concatenate([w_ref[(y * per + h) * HD : (y * per + h + 1) * HD] for y in range(nhead)], axis=0)
+        return dot(left, right)
+
+    def give_back(h):
+        await_rows(recv_x, rx_sem, h)
         attend(h)
         push(send_o, recv_o, so_sem, ro_sem, h)
         push(send_l, recv_l, sl_sem, rl_sem, h)
-    for h in range(per):
+
+    def settle(h):
         await_all(recv_o, ro_sem, h)
         await_all(recv_l, rl_sem, h)
         mix(h)
         push_heads(h)
+
+    find_seats()
+    for h in range(per):
+        await_shard(h, 0)
+    pl.semaphore_wait(barrier, nseq + nhead - 2)
+    ring_seats(0)
+    ring_shards(0, 0)
+    ring_shards(1, 0)
+    near(0, (0,))
+    for j in (1, 2):
+        await_seats(j)
+        await_shard(0, j)
+    ring_seats(1)
+    ring_shards(0, 1)
+    ring_shards(2, 0)
+    near(0, (1, 2))
+    near(1, (0,))
+    for j in (1, 2):
+        await_shard(1, j)
+    ring_shards(1, 1)
+    near(1, (1, 2))
+    for j in (3, 4):
+        await_seats(j)
+        await_shard(0, j)
+    relay(0)
+    near(2, (0,))
+    for j in (1, 2):
+        await_shard(2, j)
+    ring_shards(2, 1)
+    near(2, (1, 2))
+    for j in (3, 4):
+        await_shard(1, j)
+    relay(1)
+    give_back(0)
+    for j in (3, 4):
+        await_shard(2, j)
+    relay(2)
+    give_back(1)
+    settle(0)
+    give_back(2)
+    settle(1)
     w_copy.wait()
-    total = None
+    await_heads(rg_sem, 0)
+    total = project(0)
+    settle(2)
+    await_heads(rg_sem, 1)
+    total = total + project(1)
+    await_heads(rg_sem, 2)
+    out_ref[...] = (total + project(2)).astype(BF16)
+    part = seats.at[pl.ds(0, 4)]
+    pltpu.make_async_copy(part, part, seat_send).wait()
     for h in range(per):
-        await_heads(rg_sem, h)
-        left = jnp.concatenate([gath[h, y] for y in range(nhead)], axis=1)
-        right = jnp.concatenate([w_ref[(y * per + h) * HD : (y * per + h + 1) * HD] for y in range(nhead)], axis=0)
-        part = dot(left, right)
-        total = part if total is None else total + part
-    out_ref[...] = total.astype(BF16)
-    for h in range(per):
-        await_all(send_x, sx_sem, h)
+        part = shard.at[h, pl.ds(0, 4)]
+        pltpu.make_async_copy(part, part, ring_send.at[h]).wait()
+        await_rows(recv_x, sx_sem, h)
         await_all(send_o, so_sem, h)
         await_all(send_l, sl_sem, h)
         await_heads(sg_sem, h)
@@ -212,26 +353,32 @@
         length, width = q_in.shape
         rounds, per, _ = q_rank.shape
         cap = 2 * length // nseq
-        slots = nseq * cap
         vmem = pl.BlockSpec(memory_space=pltpu.VMEM)
+        hbm = pl.BlockSpec(memory_space=pltpu.HBM)
+        inner = nseq // PLANES
         scratch = [
             pltpu.VMEM(w_out.shape, BF16),
-            pltpu.VMEM((per, nseq, 3, rounds * cap, HD), BF16),
+            pltpu.VMEM((per, 5, 3, length, HD), BF16),
+            pltpu.VMEM((5, -(-2 * rounds * per // 8) * 8, length), F32),
+            pltpu.VMEM((per, 9, inner, 3, rounds * cap, HD), BF16),
             pltpu.VMEM((per, nseq, 3, rounds * cap, HD), BF16),
             pltpu.VMEM((per, nseq, rounds * cap, HD), BF16),
             pltpu.VMEM((per, nseq, rounds * cap, HD), BF16),
             pltpu.VMEM((per, nseq, 1, HD), F32),
             pltpu.VMEM((per, nseq, 1, HD), F32),
             pltpu.VMEM((per, nhead, length, HD), BF16),
-            pltpu.VMEM((rounds, per, slots, length), BF16),
             pltpu.VMEM((rounds, per, nseq, length), F32),
             pltpu.VMEM((rounds, per, 1, length), F32),
             pltpu.SemaphoreType.DMA,
+            pltpu.SemaphoreType.DMA,
+            pltpu.SemaphoreType.DMA((5,)),
+            pltpu.SemaphoreType.DMA((per,)),
+            pltpu.SemaphoreType.DMA((per, 5)),
         ] + [pltpu.SemaphoreType.DMA((per,))] * 8
         return pl.pallas_call(
             functools.partial(kernel, (nseq, nhead, per, rounds, length)),
             out_shape=jax.ShapeDtypeStruct((length, w_out.shape[1]), BF16),
-            in_specs=[vmem] * 5 + [pl.BlockSpec(memory_space=pl.ANY)],
+            in_specs=[hbm] * 3 + [vmem] * 2 + [hbm],
             out_specs=vmem,
             scratch_shapes=scratch,
             compiler_params=pltpu.CompilerParams(

time: 123 us -> 109 us (0.89)
  Pallas kernels: 116 us -> 102 us
    pallas_call x1, Pallas kernels: 116 us -> 102 us  [body(): pl.pallas_call(functools.partial(kernel, (nseq, nhead, per, rounds, lengt...]
where the time goes in v1:
time: 109 us; the launch traced here: 108 us
  Pallas kernels  102 us (94%)
  local copies, waits for them, and re-layouts  6.51 us (6%)
    pallas_call x1, Pallas kernels, body(): pl.pallas_call(functools.partial(kernel, (nseq, nhead, per, rounds, lengt...  102 us
    unnamed x11, local copies, waits for them, and re-layouts  6.51 us

profile of v1, /device:TPU:1, one launch (start us, length us, event | category | flops | bytes accessed | tf_op | source)
XLA Modules:
  0.0 108.2 jit_solution(11388036262920371879)
XLA Ops:
  0.0 0.7 copy.7.qrank_ref
  0.7 0.7 copy.8.krank_ref
  1.4 0.0 copy-start
  1.4 1.7 %copy-done = bf16[3072,384]{1,0:T(8,128)(2,1)S(1)} copy-done((bf16[3072,384]{1,0:T(8,128)(2,1)S(1)}, bf16[3072,384]{1,0:T(8,128)(2,1)}, u32[]{:S(2)}) %copy-start) | copy-done | bytes 2359320
  3.1 0.0 copy-start.1
  3.1 0.9 copy-done.1
  4.0 0.0 copy-start.2
  4.0 0.9 copy-done.2
  4.9 0.0 copy-start.3
  4.9 0.9 copy-done.3
  5.8 101.7 %shard_map.64 = bf16[256,384]{1,0:T(8,128)(2,1)S(1)} custom-call(bf16[256,384]{1,0:T(8,128)(2,1)S(1)} %copy-done.1, bf16[256,384]{1,0:T(8,128)(2,1)S(1)} %copy-done.2, bf16[256,384]{1,0:T(8,128)(2,1)S(1)} %copy-done.3, s32[2,3,256]{2,1,0:T(4,128)S(1)} %copy.7.qrank_ref, s32[2,3,256]{2,1,0:T(4,128)S(1)} %copy.8.krank_ref, bf16[3072,384]{1,0:T(8,128)(2,1)S(1)} %copy-done), custom_call_target="tpu_custom_call" | custom-call | tf_op jit(solution)/shard_map/pallas_call | solution.py:378
  107.5 0.7 copy.10
Async XLA Ops:
  1.4 1.7 %copy-start = (bf16[3072,384]{1,0:T(8,128)(2,1)S(1)}, bf16[3072,384]{1,0:T(8,128)(2,1)}, u32[]{:S(2)}) copy-start(bf16[3072,384]{1,0:T(8,128)(2,1)} %w_hbm.1) | copy-start | bytes 7077892
  3.1 0.9 copy-start.1
  4.0 0.9 copy-start.2
  4.9 0.9 copy-start.3

commit v2 on v1

--- a/solution.py
+++ b/solution.py
@@ -9,6 +9,7 @@
 
 MESH = pl.DeviceIdType.MESH
 HD = 128
+VMEM_BYTES = 63 * 1024 * 1024
 PLANES = 8
 EMPTY = 64.0
 F32 = jnp.float32
@@ -20,10 +21,10 @@
 
 
 def kernel(
-    sizes, q_hbm, k_hbm, v_hbm, qrank_ref, krank_ref, w_hbm, out_ref,
-    w_ref, shard, seats, packed, recv_x, send_o, recv_o, send_l, recv_l, gath, tq_ref, oq_ref,
-    w_sem, seat_send, seat_recv, ring_send, ring_recv,
-    sx_sem, rx_sem, so_sem, ro_sem, sl_sem, rl_sem, sg_sem, rg_sem,
+    sizes, q_hbm, k_hbm, v_hbm, qrank_hbm, krank_hbm, w_hbm, out_ref,
+    qrank_ref, krank_ref, w_ref, shard, seats, packed, recv_x, send_o, recv_o, send_l, recv_l, gath, tq_ref, oq_ref,
+    rank_sem, w_sem, seat_send, seat_recv, ring_send, ring_recv,
+    sx_sem, rx_sem, so_sem, ro_sem, sl_sem, rl_sem, sg_sem, rg_sem, rf_sem,
 ):
     nseq, nhead, per, rounds, length = sizes
     cap = 2 * length // nseq
@@ -48,7 +49,14 @@
     def _(step):
         pl.semaphore_signal(barrier, inc=1, device_id={"head": (my_head + step) % nhead}, device_id_type=MESH)
 
+    rank_copies = [
+        pltpu.make_async_copy(qrank_hbm, qrank_ref, rank_sem.at[0]),
+        pltpu.make_async_copy(krank_hbm, krank_ref, rank_sem.at[1]),
+    ]
     for h in range(per):
+        if h == 1:
+            for copy in rank_copies:
+                copy.start()
         for i, source in enumerate((q_hbm, k_hbm, v_hbm)):
             pltpu.make_async_copy(source.at[:, pl.ds(h * HD, HD)], shard.at[h, 0, i], ring_recv.at[h, 0]).start()
     w_copy = pltpu.make_async_copy(w_hbm, w_ref, w_sem)
@@ -64,7 +72,7 @@
         for side, rank_ref in enumerate((qrank_ref, krank_ref)):
             for r in range(rounds):
                 for h in range(per):
-                    target = rank_ref[r, h : h + 1, :] // length
+                    target = rank_ref[h, r : r + 1, :] // length
                     owner = (target == shard_ids).astype(F32)
                     before = dot(owner.astype(BF16), earlier)
                     ordinal = jnp.sum(owner * before, axis=0, keepdims=True)
@@ -250,25 +258,41 @@
         mixed = functools.reduce(jnp.add, [share / total * row for share, row in zip(shares, rows)])
         gath[h, my_head] = mixed.T.astype(BF16)
 
+    def to_head(h, owner, hop, recv_sem, rows=None):
+        part = gath.at[h, owner] if rows is None else gath.at[h, owner, rows]
+        pltpu.make_async_remote_copy(
+            src_ref=part,
+            dst_ref=part,
+            send_sem=sg_sem.at[h],
+            recv_sem=recv_sem,
+            device_id={"head": (my_head + hop + nhead) % nhead},
+            device_id_type=MESH,
+        ).start()
+
     def push_heads(h):
-        if nhead == 1:
+        if nhead != 8:
+            for hop in range(1, nhead):
+                to_head(h, my_head, hop, rg_sem.at[h])
             return
-        @pl.loop(1, nhead)
-        def _(step):
-            pltpu.make_async_remote_copy(
-                src_ref=gath.at[h, my_head],
-                dst_ref=gath.at[h, my_head],
-                send_sem=sg_sem.at[h],
-                recv_sem=rg_sem.at[h],
-                device_id={"head": (my_head + step) % nhead},
-                device_id_type=MESH,
-            ).start()
+        for i, way in enumerate((1, -1)):
+            to_head(h, my_head, 2 * way, rf_sem.at[h, i])
+        for way in (1, -1):
+            to_head(h, my_head, way, rg_sem.at[h])
+
+    def relay_heads(h):
+        if nhead != 8:
+            return
+        for i, way in enumerate((1, -1)):
+            owner = (my_head - 2 * way + nhead) % nhead
+            pltpu.make_async_copy(gath.at[h, owner], gath.at[h, owner], rf_sem.at[h, i]).wait()
+            to_head(h, owner, way, rg_sem.at[h])
+            to_head(h, owner, 2 * way, rg_sem.at[h], pl.ds(i * (length // 2), length // 2))
 
     def await_heads(sem, h):
-        if nhead == 1:
-            return
-        part = gath.at[h, pl.ds(0, nhead - 1)]
-        pltpu.make_async_copy(part, part, sem.at[h]).wait()
+        count = nhead - 1 if sem is sg_sem or nhead != 8 else nhead - 3
+        if count:
+            part = gath.at[h, pl.ds(0, count)]
+            pltpu.make_async_copy(part, part, sem.at[h]).wait()
 
     def project(h):
         left = jnp.concatenate([gath[h, y] for y in range(nhead)], axis=1)
@@ -287,13 +311,16 @@
         mix(h)
         push_heads(h)
 
+    await_shard(0, 0)
+    pl.semaphore_wait(barrier, nseq + nhead - 2)
+    ring_shards(0, 0)
+    await_shard(1, 0)
+    ring_shards(1, 0)
+    for copy in rank_copies:
+        copy.wait()
     find_seats()
-    for h in range(per):
-        await_shard(h, 0)
-    pl.semaphore_wait(barrier, nseq + nhead - 2)
     ring_seats(0)
-    ring_shards(0, 0)
-    ring_shards(1, 0)
+    await_shard(2, 0)
     near(0, (0,))
     for j in (1, 2):
         await_seats(j)
@@ -325,12 +352,15 @@
     relay(2)
     give_back(1)
     settle(0)
+    relay_heads(0)
     give_back(2)
     settle(1)
+    relay_heads(1)
     w_copy.wait()
     await_heads(rg_sem, 0)
     total = project(0)
     settle(2)
+    relay_heads(2)
     await_heads(rg_sem, 1)
     total = total + project(1)
     await_heads(rg_sem, 2)
@@ -357,6 +387,8 @@
         hbm = pl.BlockSpec(memory_space=pltpu.HBM)
         inner = nseq // PLANES
         scratch = [
+            pltpu.VMEM((per, rounds, length), jnp.int32),
+            pltpu.VMEM((per, rounds, length), jnp.int32),
             pltpu.VMEM(w_out.shape, BF16),
             pltpu.VMEM((per, 5, 3, length, HD), BF16),
             pltpu.VMEM((5, -(-2 * rounds * per // 8) * 8, length), F32),
@@ -369,22 +401,23 @@
             pltpu.VMEM((per, nhead, length, HD), BF16),
             pltpu.VMEM((rounds, per, nseq, length), F32),
             pltpu.VMEM((rounds, per, 1, length), F32),
+            pltpu.SemaphoreType.DMA((2,)),
             pltpu.SemaphoreType.DMA,
             pltpu.SemaphoreType.DMA,
             pltpu.SemaphoreType.DMA((5,)),
             pltpu.SemaphoreType.DMA((per,)),
             pltpu.SemaphoreType.DMA((per, 5)),
-        ] + [pltpu.SemaphoreType.DMA((per,))] * 8
+        ] + [pltpu.SemaphoreType.DMA((per,))] * 8 + [pltpu.SemaphoreType.DMA((per, 2))]
         return pl.pallas_call(
             functools.partial(kernel, (nseq, nhead, per, rounds, length)),
             out_shape=jax.ShapeDtypeStruct((length, w_out.shape[1]), BF16),
-            in_specs=[hbm] * 3 + [vmem] * 2 + [hbm],
+            in_specs=[hbm] * 6,
             out_specs=vmem,
             scratch_shapes=scratch,
             compiler_params=pltpu.CompilerParams(
-                collective_id=0, has_side_effects=True, vmem_limit_bytes=48 * 1024 * 1024
+                collective_id=0, has_side_effects=True, vmem_limit_bytes=VMEM_BYTES
             ),
-        )(q_in, k_in, v_in, q_rank, k_rank, w_out)
+        )(q_in, k_in, v_in, jnp.transpose(q_rank, (1, 0, 2)), jnp.transpose(k_rank, (1, 0, 2)), w_out)
 
     return jax.shard_map(
         body,

time: 109 us -> 98.3 us (0.902)
  Pallas kernels: 102 us -> 96.1 us
  local copies, waits for them, and re-layouts: 6.51 us -> 1.62 us
    pallas_call x1, Pallas kernels: 102 us -> 96.1 us  [body(): pl.pallas_call(functools.partial(kernel, (nseq, nhead, per, rounds, lengt...]
    unnamed x11 -> x1, local copies, waits for them, and re-layouts: 6.51 us -> 1.62 us
where the time goes in v2:
time: 98.3 us; the launch traced here: 97.7 us
  Pallas kernels  96.1 us (98%)
  local copies, waits for them, and re-layouts  1.62 us (2%)
    pallas_call x1, Pallas kernels, body(): pl.pallas_call(functools.partial(kernel, (nseq, nhead, per, rounds, lengt...  96.1 us

profile of v2, /device:TPU:1, one launch (start us, length us, event | category | flops | bytes accessed | tf_op | source)
XLA Modules:
  0.0 97.7 jit_solution(7562830014245393901)
XLA Ops:
  0.0 96.1 %shard_map.64 = bf16[256,384]{1,0:T(8,128)(2,1)} custom-call(bf16[256,384]{1,0:T(8,128)(2,1)} %q_hbm.1, bf16[256,384]{1,0:T(8,128)(2,1)} %k_hbm.1, bf16[256,384]{1,0:T(8,128)(2,1)} %v_hbm.1, s32[3,2,256]{2,1,0:T(2,128)} %bitcast.2, s32[3,2,256]{2,1,0:T(2,128)} %bitcast.3, bf16[3072,384]{1,0:T(8,128)(2,1)} %w_hbm.1), custom_call_target="tpu_custom_call" | custom-call | tf_op jit(solution)/shard_map/pallas_call | solution.py:411
  96.1 1.6 %copy.8 = bf16[256,384]{1,0:T(8,128)(2,1)} copy(bf16[256,384]{1,0:T(8,128)(2,1)} %shard_map.64) | data formatting | bytes 393216

commit v3 on v2

--- a/solution.py
+++ b/solution.py
@@ -41,14 +41,6 @@
     def peer_of(step):
         return plane_at(step % PLANES) * inner + (my_place + step // PLANES) % inner
 
-    @pl.loop(1, nseq)
-    def _(step):
-        pl.semaphore_signal(barrier, inc=1, device_id={"seq": peer_of(step)}, device_id_type=MESH)
-
-    @pl.loop(1, nhead)
-    def _(step):
-        pl.semaphore_signal(barrier, inc=1, device_id={"head": (my_head + step) % nhead}, device_id_type=MESH)
-
     rank_copies = [
         pltpu.make_async_copy(qrank_hbm, qrank_ref, rank_sem.at[0]),
         pltpu.make_async_copy(krank_hbm, krank_ref, rank_sem.at[1]),
@@ -59,6 +51,14 @@
                 copy.start()
         for i, source in enumerate((q_hbm, k_hbm, v_hbm)):
             pltpu.make_async_copy(source.at[:, pl.ds(h * HD, HD)], shard.at[h, 0, i], ring_recv.at[h, 0]).start()
+    @pl.loop(1, nseq)
+    def _(step):
+        pl.semaphore_signal(barrier, inc=1, device_id={"seq": peer_of(step)}, device_id_type=MESH)
+
+    @pl.loop(1, nhead)
+    def _(step):
+        pl.semaphore_signal(barrier, inc=1, device_id={"head": (my_head + step) % nhead}, device_id_type=MESH)
+
     w_copy = pltpu.make_async_copy(w_hbm, w_ref, w_sem)
     w_copy.start()
 
@@ -181,20 +181,22 @@
     def by_peer(rows):
         return rows.reshape(nseq, cap, HD)
 
-    def push(send, recv, send_sem, recv_sem, h):
-        recv[h, me] = send[h, me]
+    def push_back(h):
+        recv_o[h, me] = send_o[h, me]
+        recv_l[h, me] = send_l[h, me]
 
         @pl.loop(1, nseq)
         def _(step):
-            peer = peer_of(step)
-            pltpu.make_async_remote_copy(
-                src_ref=send.at[h, peer],
-                dst_ref=recv.at[h, me],
-                send_sem=send_sem.at[h],
-                recv_sem=recv_sem.at[h],
-                device_id={"seq": peer},
-                device_id_type=MESH,
-            ).start()
+            peer = (step - 1) + (step - 1 + nseq - me) // nseq
+            for send, recv, send_sem, recv_sem in ((send_o, recv_o, so_sem, ro_sem), (send_l, recv_l, sl_sem, rl_sem)):
+                pltpu.make_async_remote_copy(
+                    src_ref=send.at[h, peer],
+                    dst_ref=recv.at[h, me],
+                    send_sem=send_sem.at[h],
+                    recv_sem=recv_sem.at[h],
+                    device_id={"seq": peer},
+                    device_id_type=MESH,
+                ).start()
 
     def await_all(buf, sem, h):
         part = buf.at[h, pl.ds(0, nseq - 1)]
@@ -302,8 +304,7 @@
     def give_back(h):
         await_rows(recv_x, rx_sem, h)
         attend(h)
-        push(send_o, recv_o, so_sem, ro_sem, h)
-        push(send_l, recv_l, sl_sem, rl_sem, h)
+        push_back(h)
 
     def settle(h):
         await_all(recv_o, ro_sem, h)
@@ -321,28 +322,25 @@
     find_seats()
     ring_seats(0)
     await_shard(2, 0)
-    near(0, (0,))
     for j in (1, 2):
         await_seats(j)
         await_shard(0, j)
     ring_seats(1)
     ring_shards(0, 1)
     ring_shards(2, 0)
-    near(0, (1, 2))
-    near(1, (0,))
+    near(0, (0, 1, 2))
     for j in (1, 2):
         await_shard(1, j)
     ring_shards(1, 1)
-    near(1, (1, 2))
+    near(1, (0, 1, 2))
     for j in (3, 4):
         await_seats(j)
         await_shard(0, j)
     relay(0)
-    near(2, (0,))
     for j in (1, 2):
         await_shard(2, j)
     ring_shards(2, 1)
-    near(2, (1, 2))
+    near(2, (0, 1, 2))
     for j in (3, 4):
         await_shard(1, j)
     relay(1)

time: 98.3 us -> 95.6 us (0.973)
  the two profiles are of different devices: /device:TPU:1 before, /device:TPU:64 now
where the time goes in v3:
time: 95.6 us; the launch traced here: 95.5 us
  Pallas kernels  93.8 us (98%)
  local copies, waits for them, and re-layouts  1.62 us (2%)
    pallas_call x1, Pallas kernels, body(): pl.pallas_call(functools.partial(kernel, (nseq, nhead, per, rounds, lengt...  93.8 us

profile of v3, /device:TPU:64, one launch (start us, length us, event | category | flops | bytes accessed | tf_op | source)
XLA Modules:
  0.0 95.5 jit_solution(5324857538488314851)
XLA Ops:
  0.0 93.8 %shard_map.64 = bf16[256,384]{1,0:T(8,128)(2,1)} custom-call(bf16[256,384]{1,0:T(8,128)(2,1)} %q_hbm.1, bf16[256,384]{1,0:T(8,128)(2,1)} %k_hbm.1, bf16[256,384]{1,0:T(8,128)(2,1)} %v_hbm.1, s32[3,2,256]{2,1,0:T(2,128)} %bitcast.2, s32[3,2,256]{2,1,0:T(2,128)} %bitcast.3, bf16[3072,384]{1,0:T(8,128)(2,1)} %w_hbm.1), custom_call_target="tpu_custom_call" | custom-call | tf_op jit(solution)/shard_map/pallas_call | solution.py:409
  93.8 1.6 %copy.8 = bf16[256,384]{1,0:T(8,128)(2,1)} copy(bf16[256,384]{1,0:T(8,128)(2,1)} %shard_map.64) | data formatting | bytes 393216

commit v4 on v3

--- a/solution.py
+++ b/solution.py
@@ -155,7 +155,7 @@
         for j, way in ((3, 1), (4, -1)):
             source = plane_at(-2 * way) * inner + my_place
             one, two = 2 * j - 1, 2 * j
-            pack(h, j, [(my_plane, j), (plane_at(way), one), (plane_at(2 * way), two)])
+            pack(h, j, [(plane_at(way), one), (plane_at(2 * way), two)])
 
             @pl.loop(0, inner)
             def _(step):
@@ -168,11 +168,7 @@
             def _(step):
                 deliver(h, two, 2 * ((my_place // 2 + step) % half) + odd, plane_at(2 * way), source)
 
-            recv_x[h, source] = packed[h, j, my_place]
-
-            @pl.loop(1, inner)
-            def _(step):
-                deliver(h, j, (my_place + step) % inner, my_plane, source)
+        near(h, (3, 4))
 
     def await_rows(buf, sem, h):
         part = recv_x.at[h, pl.ds(0, nseq - 5)]
@@ -300,6 +296,12 @@
         left = jnp.concatenate([gath[h, y] for y in range(nhead)], axis=1)
         right = jnp.concatenate([w_ref[(y * per + h) * HD : (y * per + h + 1) * HD] for y in range(nhead)], axis=0)
         return dot(left, right)
+
+    def project_owners(h, hops):
+        owners = [(my_head + hop + nhead) % nhead for hop in hops]
+        left = jnp.concatenate([gath[h, owner] for owner in owners], axis=1)
+        starts = [pl.multiple_of((owner * per + h) * HD, HD) for owner in owners]
+        return dot(left, jnp.concatenate([w_ref[pl.ds(start, HD)] for start in starts], axis=0))
 
     def give_back(h):
         await_rows(recv_x, rx_sem, h)
@@ -361,8 +363,14 @@
     relay_heads(2)
     await_heads(rg_sem, 1)
     total = total + project(1)
-    await_heads(rg_sem, 2)
-    out_ref[...] = (total + project(2)).astype(BF16)
+    if nhead == 8:
+        total = total + project_owners(2, (0, 2, -2))
+        await_heads(rg_sem, 2)
+        total = total + project_owners(2, (1, -1, 3, -3, 4))
+    else:
+        await_heads(rg_sem, 2)
+        total = total + project(2)
+    out_ref[...] = total.astype(BF16)
     part = seats.at[pl.ds(0, 4)]
     pltpu.make_async_copy(part, part, seat_send).wait()
     for h in range(per):

time: 95.6 us -> 95.3 us (level)
  the two profiles are of different devices: /device:TPU:64 before, /device:TPU:1 now
where the time goes in v4:
time: 95.3 us; the launch traced here: 93.5 us
  Pallas kernels  91.8 us (96%)
  local copies, waits for them, and re-layouts  1.62 us (2%)
    pallas_call x1, Pallas kernels, body(): pl.pallas_call(functools.partial(kernel, (nseq, nhead, per, rounds, lengt...  91.8 us

profile of v4, /device:TPU:1, one launch (start us, length us, event | category | flops | bytes accessed | tf_op | source)
XLA Modules:
  0.0 93.5 jit_solution(13250835105295322031)
XLA Ops:
  0.0 91.8 %shard_map.64 = bf16[256,384]{1,0:T(8,128)(2,1)} custom-call(bf16[256,384]{1,0:T(8,128)(2,1)} %q_hbm.1, bf16[256,384]{1,0:T(8,128)(2,1)} %k_hbm.1, bf16[256,384]{1,0:T(8,128)(2,1)} %v_hbm.1, s32[3,2,256]{2,1,0:T(2,128)} %bitcast.2, s32[3,2,256]{2,1,0:T(2,128)} %bitcast.3, bf16[3072,384]{1,0:T(8,128)(2,1)} %w_hbm.1), custom_call_target="tpu_custom_call" | custom-call | tf_op jit(solution)/shard_map/pallas_call | solution.py:417
  91.8 1.6 %copy.8 = bf16[256,384]{1,0:T(8,128)(2,1)} copy(bf16[256,384]{1,0:T(8,128)(2,1)} %shard_map.64) | data formatting | bytes 393216
